TPU v7x, 256 devices: a whole 4x4x8 slice. The times are simulated.
256 devices in a mesh: animal: 8 (over x, core), marker: 32 (over y, z).
Axes of the slice: x: 4, y: 4, z: 8, core: 2. Of those that a mesh axis runs over, the one named last changes fastest.
Arguments:
- genotype: float32 [12288, 49152], P('animal', 'marker'), may hold values from 0 to 2, as said below
- allele_freq: float32 [49152], P('marker'), may hold values from 0.05 to 0.5
- shrink: float32 [49152], P('marker'), may hold values from 0.05 to 0.6
- right_side: float32 [32, 49152], P(None, 'marker'), may hold values from -6 to 6
Outputs:
- solution: float32 [32, 49152], P(None, 'marker')
- residual: float32 [32, 49152], P(None, 'marker')
Inputs may be any that keep to these rules, and one draw needn't show every extreme that they name: genotype codes are 0, 1 or 2.
All inputs are finite; a program needn't handle non-finite values.
Results may differ from a plain program's by a relative error of at most 0.002.
Values sent between devices are 32-bit elements; how exact they have to be, the bound alone decides.
No kernel may reach another device: no remote copies, remote signals or barrier semaphores. Data moves between devices by JAX's collectives and lax.ppermute only.
A program may use at most 64 MiB of HBM per device.

v0:
```python
import jax
import jax.numpy as jnp
from jax import lax
from jax.sharding import PartitionSpec as P

ITERS = 4


def body(genotype, allele_freq, shrink, right_side):
    a_rows = genotype.shape[0]
    count = jnp.float32(a_rows * lax.axis_size("animal"))
    inv_count = jnp.float32(1.0) / count
    precond_full = 2.0 * allele_freq * (1.0 - allele_freq) + shrink
    freq_own, shrink_own, precond = (allele_freq, shrink, precond_full)
    residual = right_side

    def inner(left, right):
        local_dot = jnp.sum(left * right, axis=1)
        return lax.psum(local_dot, "marker")

    solution = jnp.zeros_like(residual)
    scaled = residual / precond[None, :]
    direction = scaled
    rho_now = inner(residual, scaled)
    for step in range(ITERS):
        offset = jnp.sum(2.0 * allele_freq[None, :] * direction, axis=1)
        partial_value = (
            lax.dot_general(
                direction,
                genotype,
                (((1,), (1,)), ((), ())),
                precision=lax.Precision.HIGHEST,
                preferred_element_type=jnp.float32,
            )
            - offset[:, None]
        )
        row_values = lax.psum(partial_value, "marker")
        col_part = jnp.dot(
            row_values,
            genotype,
            precision=lax.Precision.HIGHEST,
            preferred_element_type=jnp.float32,
        )
        row_total = jnp.sum(row_values, axis=1)
        col_part, row_total = (col_part, row_total)
        col_terms, row_sum = lax.psum((col_part, row_total), "animal")
        image = (col_terms - 2.0 * freq_own[None, :] * row_sum[:, None]) * inv_count + shrink_own[
            None, :
        ] * direction
        curve = inner(direction, image)
        step_len = rho_now / curve
        solution = solution + step_len[:, None] * direction
        residual = residual - step_len[:, None] * image
        scaled = residual / precond[None, :]
        rho_new = inner(residual, scaled)
        direction = scaled + (rho_new / rho_now)[:, None] * direction
        rho_now = rho_new
    return (solution, residual)


def solution(mesh):
    placed = (P("animal", "marker"), P("marker"), P("marker"), P(None, "marker"))
    return jax.shard_map(
        body,
        mesh=mesh,
        in_specs=placed,
        out_specs=(P(None, "marker"), P(None, "marker")),
        check_vma=False,
    )
```

profile of v0, /device:TPU:0, one launch (start us, length us, event | category | flops | bytes accessed | tf_op | source)
XLA Modules:
  0.0 1424.5 jit_solution(13749185263158881050)
XLA Ops:
  9.0 13.0 convolution_subtract_fusion.3
  22.1 143.9 %all-reduce.10.cloned.1.call-done = f32[32,1536]{1,0:T(8,128)} async-done(((f32[32,1536]{1,0:T(8,128)}), f32[32,1536]{1,0:T(8,128)}) %all-reduce.10.cloned.1.call-update) | async-done | bytes 196624 | tf_op jit(solution)/shard_map/psum | solution.py:37
  176.1 12.4 psum.143
  188.5 49.8 %all-reduce.12.cloned.1.call-done = f32[32,1536]{1,0:T(8,128)} async-done(((f32[32,1536]{1,0:T(8,128)}), f32[32,1536]{1,0:T(8,128)}) %all-reduce.12.cloned.1.call-update) | async-done | bytes 196624 | tf_op jit(solution)/shard_map/psum | solution.py:46
  239.4 75.6 %all-reduce = (f32[32]{0:T(128)S(1)}, f32[32]{0:T(128)S(1)}) all-reduce(f32[32]{0:T(128)S(1)} %get-tuple-element.3, f32[32]{0:T(128)S(1)} %get-tuple-element.2), channel_id=1, replica_groups=mesh['animal'=8,'marker'=32] {'marker'}, use_global_device_ids=true, to_apply=%region_1.0 | all-reduce | flops 64 | bytes 512 | tf_op jit(solution)/shard_map/psum | solution.py:19
  316.2 69.7 %psum.145 = f32[32]{0:T(128)S(1)} all-reduce(f32[32]{0:T(128)S(1)} %get-tuple-element.16), channel_id=1, replica_groups=mesh['animal'=8,'marker'=32] {'marker'}, use_global_device_ids=true, to_apply=%region_10.0 | all-reduce | flops 32 | bytes 256 | tf_op jit(solution)/shard_map/psum | solution.py:19
  386.1 11.7 convolution_subtract_fusion.2
  397.8 135.4 %all-reduce.14.cloned.1.call-done = f32[32,1536]{1,0:T(8,128)} async-done(((f32[32,1536]{1,0:T(8,128)}), f32[32,1536]{1,0:T(8,128)}) %all-reduce.14.cloned.1.call-update) | async-done | bytes 196624 | tf_op jit(solution)/shard_map/psum | solution.py:37
  533.2 10.0 fusion.1
  543.4 12.4 psum.148
  555.8 49.7 %all-reduce.16.cloned.1.call-done = f32[32,1536]{1,0:T(8,128)} async-done(((f32[32,1536]{1,0:T(8,128)}), f32[32,1536]{1,0:T(8,128)}) %all-reduce.16.cloned.1.call-update) | async-done | bytes 196624 | tf_op jit(solution)/shard_map/psum | solution.py:46
  606.7 75.1 %psum.149 = f32[32]{0:T(128)S(1)} all-reduce(f32[32]{0:T(128)S(1)} %multiply_reduce_fusion.6), channel_id=1, replica_groups=mesh['animal'=8,'marker'=32] {'marker'}, use_global_device_ids=true, to_apply=%region_17.0 | all-reduce | flops 32 | bytes 256 | tf_op jit(solution)/shard_map/psum | solution.py:19
  683.0 69.8 %psum.150 = f32[32]{0:T(128)S(1)} all-reduce(f32[32]{0:T(128)S(1)} %get-tuple-element.12), channel_id=1, replica_groups=mesh['animal'=8,'marker'=32] {'marker'}, use_global_device_ids=true, to_apply=%region_19.0 | all-reduce | flops 32 | bytes 256 | tf_op jit(solution)/shard_map/psum | solution.py:19
  753.0 11.7 convolution_subtract_fusion.1
  764.7 135.4 %all-reduce.18.cloned.1.call-done = f32[32,1536]{1,0:T(8,128)} async-done(((f32[32,1536]{1,0:T(8,128)}), f32[32,1536]{1,0:T(8,128)}) %all-reduce.18.cloned.1.call-update) | async-done | bytes 196624 | tf_op jit(solution)/shard_map/psum | solution.py:37
  910.3 12.4 psum.153
  922.7 49.7 %all-reduce.20.cloned.1.call-done = f32[32,1536]{1,0:T(8,128)} async-done(((f32[32,1536]{1,0:T(8,128)}), f32[32,1536]{1,0:T(8,128)}) %all-reduce.20.cloned.1.call-update) | async-done | bytes 196624 | tf_op jit(solution)/shard_map/psum | solution.py:46
  973.6 75.1 %psum.154 = f32[32]{0:T(128)S(1)} all-reduce(f32[32]{0:T(128)S(1)} %multiply_reduce_fusion.3), channel_id=1, replica_groups=mesh['animal'=8,'marker'=32] {'marker'}, use_global_device_ids=true, to_apply=%region_26.0 | all-reduce | flops 32 | bytes 256 | tf_op jit(solution)/shard_map/psum | solution.py:19
  1049.8 69.8 %psum.155 = f32[32]{0:T(128)S(1)} all-reduce(f32[32]{0:T(128)S(1)} %get-tuple-element.8), channel_id=1, replica_groups=mesh['animal'=8,'marker'=32] {'marker'}, use_global_device_ids=true, to_apply=%region_28.0 | all-reduce | flops 32 | bytes 256 | tf_op jit(solution)/shard_map/psum | solution.py:19
  1119.9 11.7 convolution_subtract_fusion
  1131.6 135.4 %all-reduce.22.cloned.1.call-done = f32[32,1536]{1,0:T(8,128)} async-done(((f32[32,1536]{1,0:T(8,128)}), f32[32,1536]{1,0:T(8,128)}) %all-reduce.22.cloned.1.call-update) | async-done | bytes 196624 | tf_op jit(solution)/shard_map/psum | solution.py:37
  1277.2 12.4 psum.158
  1289.6 49.8 %all-reduce.24.cloned.1.call-done = f32[32,1536]{1,0:T(8,128)} async-done(((f32[32,1536]{1,0:T(8,128)}), f32[32,1536]{1,0:T(8,128)}) %all-reduce.24.cloned.1.call-update) | async-done | bytes 196624 | tf_op jit(solution)/shard_map/psum | solution.py:46
  1340.5 75.1 %psum.159 = f32[32]{0:T(128)S(1)} all-reduce(f32[32]{0:T(128)S(1)} %multiply_reduce_fusion), channel_id=1, replica_groups=mesh['animal'=8,'marker'=32] {'marker'}, use_global_device_ids=true, to_apply=%region_35.0 | all-reduce | flops 32 | bytes 256 | tf_op jit(solution)/shard_map/psum | solution.py:19
  (55 shorter events, 43.2 us)
Async XLA Ops:
  7.2 158.8 %all-reduce.10.cloned.1.call-start = ((), (), s32[]{:S(2)}) async-start(), calls=%async_computation | async-start | bytes 393216 | tf_op jit(solution)/shard_map/psum | solution.py:37
  9.0 229.3 %copy-start = (f32[32,1536]{1,0:T(8,128)S(1)}, f32[32,1536]{1,0:T(8,128)}, u32[]{:S(2)}) copy-start(f32[32,1536]{1,0:T(8,128)} %param.7) | copy-start | bytes 589828
  9.0 229.3 %copy-start.5 = (f32[1536]{0:T(1024)S(1)}, f32[1536]{0:T(1024)}, u32[]{:S(2)}) copy-start(f32[1536]{0:T(1024)} %param.6) | copy-start | bytes 18436
  22.0 216.3 %all-reduce.12.cloned.1.call-start = ((), (), s32[]{:S(2)}) async-start(), calls=%async_computation.1 | async-start | bytes 393216 | tf_op jit(solution)/shard_map/psum | solution.py:46
  166.0 10.0 copy-start.1
  175.9 357.3 %all-reduce.14.cloned.1.call-start = ((), (), s32[]{:S(2)}) async-start(), calls=%async_computation.2 | async-start | bytes 393216 | tf_op jit(solution)/shard_map/psum | solution.py:37
  397.8 207.8 %all-reduce.16.cloned.1.call-start = ((), (), s32[]{:S(2)}) async-start(), calls=%async_computation.3 | async-start | bytes 393216 | tf_op jit(solution)/shard_map/psum | solution.py:46
  533.2 10.0 copy-start.2
  543.2 356.9 %all-reduce.18.cloned.1.call-start = ((), (), s32[]{:S(2)}) async-start(), calls=%async_computation.4 | async-start | bytes 393216 | tf_op jit(solution)/shard_map/psum | solution.py:37
  764.7 207.7 %all-reduce.20.cloned.1.call-start = ((), (), s32[]{:S(2)}) async-start(), calls=%async_computation.5 | async-start | bytes 393216 | tf_op jit(solution)/shard_map/psum | solution.py:46
  900.1 10.0 copy-start.3
  910.1 357.0 %all-reduce.22.cloned.1.call-start = ((), (), s32[]{:S(2)}) async-start(), calls=%async_computation.6 | async-start | bytes 393216 | tf_op jit(solution)/shard_map/psum | solution.py:37
  1131.6 207.8 %all-reduce.24.cloned.1.call-start = ((), (), s32[]{:S(2)}) async-start(), calls=%async_computation.7 | async-start | bytes 393216 | tf_op jit(solution)/shard_map/psum | solution.py:46
  1267.1 10.0 copy-start.4
Sparse Core Ops, SparseCore 0:
  22.1 143.7 all-reduce.9
  176.1 62.1 all-reduce.11
  397.9 135.2 all-reduce.13
  543.3 62.1 all-reduce.15
  764.8 135.2 all-reduce.17
  910.2 62.1 all-reduce.19
  1131.7 135.2 all-reduce.21
  1277.2 62.1 all-reduce.23
where the time goes:
time: 1430 us; the launch traced here: 1420 us
  waiting for transfers between devices  749 us (52%)
  blocking collectives  560 us (39%)
  matrix products  87.8 us (6%)
  between operations  14.4 us (1%)
    psum x4, waiting for transfers between devices, body(): row_values = lax.psum(partial_value, 'marker')  550 us
    psum x7, blocking collectives, inner(): return lax.psum(local_dot, 'marker')  510 us
    psum x4, waiting for transfers between devices, body(): col_terms, row_sum = lax.psum((col_part, row_total), 'animal')  199 us
    psum x4, blocking collectives, body(): col_terms, row_sum = lax.psum((col_part, row_total), 'animal')  49.7 us
    dot_general x4, matrix products, body(): lax.dot_general(direction, genotype, (((1,), (1,)), ((), ())), precision=...  48 us
    dot_general x4, matrix products, body(): jnp.dot(row_values, genotype, precision=lax.Precision.HIGHEST, preferred_...  39.8 us
  transfers between devices with their start and end apart: 8, of which 8 were waited for; matrix products, arithmetic and copies ran while one was open for 0% of the time, Pallas kernels for 0%

commit v1 on v0

--- a/solution.py
+++ b/solution.py
@@ -34,7 +34,8 @@
             )
             - offset[:, None]
         )
-        row_values = lax.psum(partial_value, "marker")
+        pieces = lax.all_gather(partial_value, "marker", axis=0, tiled=False)
+        row_values = pieces.sum(axis=0)
         col_part = jnp.dot(
             row_values,
             genotype,

time: 1430 us -> 1210 us (0.85)
  waiting for transfers between devices: 749 us -> 512 us
  other arithmetic: 12.9 us -> 37.6 us
    psum x4 -> x0, waiting for transfers between devices: 550 us -> none  [body(): row_values = lax.psum(partial_value, 'marker')]
    all_gather x0 -> x4, waiting for transfers between devices: none -> 334 us  [body(): pieces = lax.all_gather(partial_value, 'marker', axis=0, tiled=False)]
    psum x4, waiting for transfers between devices: 199 us -> 178 us  [body(): col_terms, row_sum = lax.psum((col_part, row_total), 'animal')]
  transfers between devices with their start and end apart: 8 -> 8, of which waited for: 8 -> 8; matrix products, arithmetic and copies ran while one was open for 0% -> 1% of each run, Pallas kernels for 0% -> 0%
where the time goes in v1:
time: 1210 us
  blocking collectives  566 us (47%)
  waiting for transfers between devices  512 us (42%)
  matrix products  82.3 us (7%)
  other arithmetic  37.6 us (3%)
  between operations  14.2 us (1%)
    psum x7, blocking collectives, inner(): return lax.psum(local_dot, 'marker')  510 us
    all_gather x4, waiting for transfers between devices, body(): pieces = lax.all_gather(partial_value, 'marker', axis=0, tiled=False)  334 us
    psum x4, waiting for transfers between devices, body(): col_terms, row_sum = lax.psum((col_part, row_total), 'animal')  178 us
    psum x4, blocking collectives, body(): col_terms, row_sum = lax.psum((col_part, row_total), 'animal')  56.6 us
    dot_general x4, matrix products, body(): lax.dot_general(direction, genotype, (((1,), (1,)), ((), ())), precision=...  47.9 us
    dot_general x4, matrix products, body(): jnp.dot(row_values, genotype, precision=lax.Precision.HIGHEST, preferred_...  34.4 us
  transfers between devices with their start and end apart: 8, of which 8 were waited for; matrix products, arithmetic and copies ran while one was open for 1% of the time, Pallas kernels for 0%

profile of v1, /device:TPU:0, one launch (start us, length us, event | category | flops | bytes accessed | tf_op | source)
XLA Modules:
  0.0 1213.1 jit_solution(11488606552514976017)
XLA Ops:
  9.0 12.9 %convolution_subtract_fusion.3 = f32[32,1536]{1,0:T(8,128)} fusion(f32[1536,1536]{1,0:T(8,128)} %param.4, f32[32]{0:T(128)S(1)} %multiply_reduce_fusion.10, f32[32,1536]{1,0:T(8,128)} %param.7, f32[1536]{0:T(1024)S(1)} %get-tuple-element.20), kind=kOutput, calls=%fused_computation.3 | convolution fusion | flops 906067968 | bytes 9836672 | tf_op jit(solution)/shard_map/dot_general | solution.py:28
  22.0 90.1 %all-gather.9.cloned.1.call-done = f32[1024,1536]{1,0:T(8,128)} async-done(((f32[32,1536]{1,0:T(8,128)}), f32[1024,1536]{1,0:T(8,128)}) %all-gather.9.cloned.1.call-update) | async-done | bytes 6291472 | tf_op jit(solution)/shard_map/all_gather | solution.py:37
  115.2 8.6 fusion
  127.2 14.2 %psum.114 = f32[32]{0:T(128)S(1)} all-reduce(f32[32]{0:T(128)S(1)} %reduce_sum.183), channel_id=1, replica_groups=mesh['animal'=8,'marker'=32] {'animal'}, use_global_device_ids=true, to_apply=%region_6.0 | all-reduce | flops 32 | bytes 256 | tf_op jit(solution)/shard_map/psum | solution.py:47
  141.3 44.4 %all-reduce.6.cloned.1.call-done = f32[32,1536]{1,0:T(8,128)} async-done(((f32[32,1536]{1,0:T(8,128)}), f32[32,1536]{1,0:T(8,128)}) %all-reduce.6.cloned.1.call-update) | async-done | bytes 196624 | tf_op jit(solution)/shard_map/psum | solution.py:47
  186.8 75.1 %all-reduce = (f32[32]{0:T(128)S(1)}, f32[32]{0:T(128)S(1)}) all-reduce(f32[32]{0:T(128)S(1)} %get-tuple-element.3, f32[32]{0:T(128)S(1)} %get-tuple-element.2), channel_id=1, replica_groups=mesh['animal'=8,'marker'=32] {'marker'}, use_global_device_ids=true, to_apply=%region_1.0 | all-reduce | flops 64 | bytes 512 | tf_op jit(solution)/shard_map/psum | solution.py:19
  263.1 69.8 %psum.116 = f32[32]{0:T(128)S(1)} all-reduce(f32[32]{0:T(128)S(1)} %get-tuple-element.16), channel_id=1, replica_groups=mesh['animal'=8,'marker'=32] {'marker'}, use_global_device_ids=true, to_apply=%region_10.0 | all-reduce | flops 32 | bytes 256 | tf_op jit(solution)/shard_map/psum | solution.py:19
  333.2 11.7 convolution_subtract_fusion.2
  344.9 81.5 %all-gather.11.cloned.1.call-done = f32[1024,1536]{1,0:T(8,128)} async-done(((f32[32,1536]{1,0:T(8,128)}), f32[1024,1536]{1,0:T(8,128)}) %all-gather.11.cloned.1.call-update) | async-done | bytes 6291472 | tf_op jit(solution)/shard_map/all_gather | solution.py:37
  441.5 14.1 %psum.118 = f32[32]{0:T(128)S(1)} all-reduce(f32[32]{0:T(128)S(1)} %reduce_sum.188), channel_id=1, replica_groups=mesh['animal'=8,'marker'=32] {'animal'}, use_global_device_ids=true, to_apply=%region_15.0 | all-reduce | flops 32 | bytes 256 | tf_op jit(solution)/shard_map/psum | solution.py:47
  455.6 44.4 %all-reduce.8.cloned.1.call-done = f32[32,1536]{1,0:T(8,128)} async-done(((f32[32,1536]{1,0:T(8,128)}), f32[32,1536]{1,0:T(8,128)}) %all-reduce.8.cloned.1.call-update) | async-done | bytes 196624 | tf_op jit(solution)/shard_map/psum | solution.py:47
  501.1 75.1 %psum.119 = f32[32]{0:T(128)S(1)} all-reduce(f32[32]{0:T(128)S(1)} %multiply_reduce_fusion.6), channel_id=1, replica_groups=mesh['animal'=8,'marker'=32] {'marker'}, use_global_device_ids=true, to_apply=%region_17.0 | all-reduce | flops 32 | bytes 256 | tf_op jit(solution)/shard_map/psum | solution.py:19
  577.4 69.7 %psum.120 = f32[32]{0:T(128)S(1)} all-reduce(f32[32]{0:T(128)S(1)} %get-tuple-element.12), channel_id=1, replica_groups=mesh['animal'=8,'marker'=32] {'marker'}, use_global_device_ids=true, to_apply=%region_19.0 | all-reduce | flops 32 | bytes 256 | tf_op jit(solution)/shard_map/psum | solution.py:19
  647.3 11.7 convolution_subtract_fusion.1
  659.3 81.3 %all-gather.13.cloned.1.call-done = f32[1024,1536]{1,0:T(8,128)} async-done(((f32[32,1536]{1,0:T(8,128)}), f32[1024,1536]{1,0:T(8,128)}) %all-gather.13.cloned.1.call-update) | async-done | bytes 6291472 | tf_op jit(solution)/shard_map/all_gather | solution.py:37
  755.6 14.1 %psum.122 = f32[32]{0:T(128)S(1)} all-reduce(f32[32]{0:T(128)S(1)} %reduce_sum.193), channel_id=1, replica_groups=mesh['animal'=8,'marker'=32] {'animal'}, use_global_device_ids=true, to_apply=%region_24.0 | all-reduce | flops 32 | bytes 256 | tf_op jit(solution)/shard_map/psum | solution.py:47
  769.7 44.4 %all-reduce.10.cloned.1.call-done = f32[32,1536]{1,0:T(8,128)} async-done(((f32[32,1536]{1,0:T(8,128)}), f32[32,1536]{1,0:T(8,128)}) %all-reduce.10.cloned.1.call-update) | async-done | bytes 196624 | tf_op jit(solution)/shard_map/psum | solution.py:47
  815.2 75.1 %psum.123 = f32[32]{0:T(128)S(1)} all-reduce(f32[32]{0:T(128)S(1)} %multiply_reduce_fusion.3), channel_id=1, replica_groups=mesh['animal'=8,'marker'=32] {'marker'}, use_global_device_ids=true, to_apply=%region_26.0 | all-reduce | flops 32 | bytes 256 | tf_op jit(solution)/shard_map/psum | solution.py:19
  891.5 69.7 %psum.124 = f32[32]{0:T(128)S(1)} all-reduce(f32[32]{0:T(128)S(1)} %get-tuple-element.8), channel_id=1, replica_groups=mesh['animal'=8,'marker'=32] {'marker'}, use_global_device_ids=true, to_apply=%region_28.0 | all-reduce | flops 32 | bytes 256 | tf_op jit(solution)/shard_map/psum | solution.py:19
  961.4 11.7 convolution_subtract_fusion
  973.1 81.5 %all-gather.15.cloned.1.call-done = f32[1024,1536]{1,0:T(8,128)} async-done(((f32[32,1536]{1,0:T(8,128)}), f32[1024,1536]{1,0:T(8,128)}) %all-gather.15.cloned.1.call-update) | async-done | bytes 6291472 | tf_op jit(solution)/shard_map/all_gather | solution.py:37
  1069.6 14.1 %psum.126 = f32[32]{0:T(128)S(1)} all-reduce(f32[32]{0:T(128)S(1)} %reduce_sum.198), channel_id=1, replica_groups=mesh['animal'=8,'marker'=32] {'animal'}, use_global_device_ids=true, to_apply=%region_33.0 | all-reduce | flops 32 | bytes 256 | tf_op jit(solution)/shard_map/psum | solution.py:47
  1083.8 44.4 %all-reduce.12.cloned.1.call-done = f32[32,1536]{1,0:T(8,128)} async-done(((f32[32,1536]{1,0:T(8,128)}), f32[32,1536]{1,0:T(8,128)}) %all-reduce.12.cloned.1.call-update) | async-done | bytes 196624 | tf_op jit(solution)/shard_map/psum | solution.py:47
  1129.3 75.1 %psum.127 = f32[32]{0:T(128)S(1)} all-reduce(f32[32]{0:T(128)S(1)} %multiply_reduce_fusion), channel_id=1, replica_groups=mesh['animal'=8,'marker'=32] {'marker'}, use_global_device_ids=true, to_apply=%region_35.0 | all-reduce | flops 32 | bytes 256 | tf_op jit(solution)/shard_map/psum | solution.py:19
  (59 shorter events, 64.3 us)
Async XLA Ops:
  7.2 104.9 %all-gather.9.cloned.1.call-start = ((), (), s32[]{:S(2)}) async-start(), calls=%async_computation.4 | async-start | bytes 6488064 | tf_op jit(solution)/shard_map/all_gather | solution.py:37
  22.0 163.7 %all-reduce.6.cloned.1.call-start = ((), (), s32[]{:S(2)}) async-start(), calls=%async_computation | async-start | bytes 393216 | tf_op jit(solution)/shard_map/psum | solution.py:47
  115.2 70.5 %copy-start = (f32[32,1536]{1,0:T(8,128)S(1)}, f32[32,1536]{1,0:T(8,128)}, u32[]{:S(2)}) copy-start(f32[32,1536]{1,0:T(8,128)} %param.7) | copy-start | bytes 589828
  115.2 70.5 %copy-start.1 = (f32[1536]{0:T(1024)S(1)}, f32[1536]{0:T(1024)}, u32[]{:S(2)}) copy-start(f32[1536]{0:T(1024)} %param.6) | copy-start | bytes 18436
  123.9 302.6 %all-gather.11.cloned.1.call-start = ((), (), s32[]{:S(2)}) async-start(), calls=%async_computation.5 | async-start | bytes 6488064 | tf_op jit(solution)/shard_map/all_gather | solution.py:37
  344.8 155.1 %all-reduce.8.cloned.1.call-start = ((), (), s32[]{:S(2)}) async-start(), calls=%async_computation.1 | async-start | bytes 393216 | tf_op jit(solution)/shard_map/psum | solution.py:47
  438.2 302.4 %all-gather.13.cloned.1.call-start = ((), (), s32[]{:S(2)}) async-start(), calls=%async_computation.6 | async-start | bytes 6488064 | tf_op jit(solution)/shard_map/all_gather | solution.py:37
  659.0 155.1 %all-reduce.10.cloned.1.call-start = ((), (), s32[]{:S(2)}) async-start(), calls=%async_computation.2 | async-start | bytes 393216 | tf_op jit(solution)/shard_map/psum | solution.py:47
  752.3 302.4 %all-gather.15.cloned.1.call-start = ((), (), s32[]{:S(2)}) async-start(), calls=%async_computation.7 | async-start | bytes 6488064 | tf_op jit(solution)/shard_map/all_gather | solution.py:37
  973.1 155.1 %all-reduce.12.cloned.1.call-start = ((), (), s32[]{:S(2)}) async-start(), calls=%async_computation.3 | async-start | bytes 393216 | tf_op jit(solution)/shard_map/psum | solution.py:47
Sparse Core Ops, SparseCore 0:
  22.1 89.9 all-gather.8
  124.0 61.6 all-reduce.5
  345.0 81.4 all-gather.10
  438.3 61.6 all-reduce.7
  659.1 81.3 all-gather.12
  752.4 61.6 all-reduce.9
  973.2 81.3 all-gather.14
  1066.5 61.6 all-reduce.11
